TPU v7x, 32 devices: a whole 2x2x4 slice. The times are simulated.
32 devices in a mesh: dom: 2 (over y), energy: 16 (over z, x, core).
Axes of the slice: x: 2, y: 2, z: 4, core: 2. Of those that a mesh axis runs over, the one named last changes fastest.
Arguments:
- hamiltonian: float32 [2, 128, 128], P('dom'), may hold values from -0.5 to 0.5
- coupling: float32 [2, 64, 64], P('dom'), may hold values from -0.75 to 0.75
- contact_rates: float32 [2, 64], replicated, may hold values from 0.2 to 2
- occupation: float32 [1, 16, 2], P(None, 'energy'), may hold values from 0 to 1
- lesser_in: float32 [1, 16, 2, 2, 128, 128], P(None, 'energy', 'dom'), may hold values from -1 to 1, as said below
- greater_in: float32 [1, 16, 2, 2, 128, 128], P(None, 'energy', 'dom'), may hold values from -1 to 1, as said below
- phonon_shift: int32 [1], replicated, may hold values from 1 to 7
Outputs:
- lesser_out: float32 [1, 16, 2, 2, 128, 128], P(None, 'energy', 'dom')
- greater_out: float32 [1, 16, 2, 2, 128, 128], P(None, 'energy', 'dom')
Inputs may be any that keep to these rules, and one draw needn't show every extreme that they name: Each block of lesser_in is i times a Hermitian positive semidefinite matrix. Each block of greater_in is -i times a Hermitian positive semidefinite matrix. phonon_shift is below 8.
All inputs are finite; a program needn't handle non-finite values.
Results may differ from a plain program's by a relative error of at most 0.00027.
Values sent between devices are 32-bit elements; how exact they have to be, the bound alone decides.
A program may use at most 64 MiB of HBM per device.

v0:
```python
import functools

import jax
import jax.numpy as jnp
from jax import lax
from jax.experimental import pallas as pl
from jax.experimental.pallas import tpu as pltpu
from jax.sharding import PartitionSpec as P

QUANTUM_BITS = 6


highest = lax.Precision.HIGHEST
broadening = 0.2
phonon_bose = 0.4
phonon_strength = 0.5


def shifted(value, axis, steps):
    count = lax.axis_size(axis)
    leading, last = (max(0, -steps), min(count, count - steps))
    return lax.ppermute(value, axis, [(source, source + steps) for source in range(leading, last)])


def from_behind(value, axis, steps):
    count = lax.axis_size(axis)
    pairs = [(source, (source + steps) % count) for source in range(count)]
    return lax.ppermute(value, axis, pairs)


def matmul_high(first_factor, second_factor):
    return jnp.matmul(first_factor, second_factor, precision=highest)


def transposed(matrix):
    return jnp.swapaxes(matrix, -1, -2)


def complex_product(first_pair, second_pair):
    return (
        matmul_high(first_pair[0], second_pair[0]) - matmul_high(first_pair[1], second_pair[1]),
        matmul_high(first_pair[0], second_pair[1]) + matmul_high(first_pair[1], second_pair[0]),
    )


def adjoint(complex_pair):
    return (transposed(complex_pair[0]), -transposed(complex_pair[1]))


def inverted(complex_pair):
    real_part, imag_part = complex_pair
    orbitals = real_part.shape[-1]
    normal_real = matmul_high(transposed(real_part), real_part) + matmul_high(
        transposed(imag_part), imag_part
    )
    normal_imag = matmul_high(transposed(real_part), imag_part) - matmul_high(
        transposed(imag_part), real_part
    )
    stacked = jnp.concatenate(
        [
            jnp.concatenate([normal_real, -normal_imag], -1),
            jnp.concatenate([normal_imag, normal_real], -1),
        ],
        -2,
    )
    factor = jnp.linalg.cholesky(stacked)
    right_side = jnp.concatenate([transposed(real_part), -transposed(imag_part)], -2)
    middle = lax.linalg.triangular_solve(factor, right_side, left_side=True, lower=True)
    solved = lax.linalg.triangular_solve(
        factor, middle, left_side=True, lower=True, transpose_a=True
    )
    return (solved[..., :orbitals, :], solved[..., orbitals:, :])


def pad_first(corner, orbitals):
    extra = orbitals - corner.shape[-1]
    return jnp.pad(corner, ((0, 0), (0, extra), (0, extra)))


def pad_last(corner, orbitals):
    extra = orbitals - corner.shape[-1]
    return jnp.pad(corner, ((0, 0), (extra, 0), (extra, 0)))


def settle(runner, stored, inbound, outbound, active):
    return lax.cond(active, lambda: runner(inbound), lambda: (stored, outbound))


def pass_right(outbound):
    return shifted(outbound, "dom", 1)


def pass_left(outbound):
    return shifted(outbound, "dom", -1)


def on_device(
    hamiltonian, coupling, contact_rates, occupation, lesser_in, greater_in, phonon_shift
):
    dom_index = lax.axis_index("dom")
    dom_count = lax.axis_size("dom")
    energy_index = lax.axis_index("energy")
    energy_count = lax.axis_size("energy")
    local_energies = occupation.shape[0]
    local_blocks = hamiltonian.shape[0]
    orbitals = hamiltonian.shape[1]
    interface = coupling.shape[1]
    total_energies = local_energies * energy_count
    global_energy = jnp.arange(local_energies, dtype=jnp.int32) * energy_count + energy_index
    energy_value = -1.5 + 3.0 * global_energy.astype(jnp.float32) / (total_energies - 1)
    identity = jnp.eye(orbitals, dtype=jnp.float32)
    extra = orbitals - interface
    gamma_left = jnp.pad(jnp.diag(contact_rates[0]), ((0, extra), (0, extra)))
    last_coupling = coupling[local_blocks - 1]
    gamma_right = jnp.pad(
        matmul_high(last_coupling * contact_rates[1][None, :], transposed(last_coupling)),
        ((extra, 0), (extra, 0)),
    )
    at_left = (dom_index == 0).astype(jnp.float32)
    at_right = (dom_index == dom_count - 1).astype(jnp.float32)

    def system(position):
        onsite = 0.5 * (hamiltonian[position] + hamiltonian[position].T)
        lesser_block = lesser_in[:, 0, position]
        greater_block = greater_in[:, 0, position]
        matrix_real = (
            energy_value[:, None, None] * identity
            - onsite
            - 0.5 * (greater_block[:, 0] - lesser_block[:, 0])
        )
        matrix_imag = broadening * identity - 0.5 * (greater_block[:, 1] - lesser_block[:, 1])
        source_imag = lesser_block[:, 1]
        matrix_imag = matrix_imag + 0.5 * at_left * gamma_left
        source_imag = source_imag + at_left * occupation[:, 0, 0, None, None] * gamma_left
        matrix_imag = matrix_imag + 0.5 * at_right * gamma_right
        source_imag = source_imag + at_right * occupation[:, 0, 1, None, None] * gamma_right
        return ((matrix_real, matrix_imag), (lesser_block[:, 0], source_imag))

    def trailing(green_block, lesser_block):
        return jnp.stack(
            [
                green_block[0][..., -interface:, -interface:],
                green_block[1][..., -interface:, -interface:],
                lesser_block[0][..., -interface:, -interface:],
                lesser_block[1][..., -interface:, -interface:],
            ]
        )

    def leading(green_block, lesser_block):
        return jnp.stack(
            [
                green_block[0][..., :interface, :interface],
                green_block[1][..., :interface, :interface],
                lesser_block[0][..., :interface, :interface],
                lesser_block[1][..., :interface, :interface],
            ]
        )

    def left_sweep(inbound):
        boundary = inbound
        matrix, source = system(0)
        matrix = (
            matrix[0] - pad_first(boundary[0], orbitals),
            matrix[1] - pad_first(boundary[1], orbitals),
        )
        source = (
            source[0] + pad_first(boundary[2], orbitals),
            source[1] + pad_first(boundary[3], orbitals),
        )
        green_block = inverted(matrix)
        lesser_block = complex_product(complex_product(green_block, source), adjoint(green_block))
        kept_blocks = [boundary]
        link_block = coupling[0]
        boundary = matmul_high(
            transposed(link_block), matmul_high(trailing(green_block, lesser_block), link_block)
        )
        return (jnp.stack(kept_blocks, 2), boundary)

    def right_sweep(inbound):
        corner = inbound
        kept_blocks = [None] * local_blocks
        for position in reversed(range(local_blocks)):
            link_block = coupling[position]
            boundary = matmul_high(link_block, matmul_high(corner, transposed(link_block)))
            matrix, source = system(position)
            matrix = (
                matrix[0] - pad_last(boundary[0], orbitals),
                matrix[1] - pad_last(boundary[1], orbitals),
            )
            source = (
                source[0] + pad_last(boundary[2], orbitals),
                source[1] + pad_last(boundary[3], orbitals),
            )
            green_block = inverted(matrix)
            lesser_block = complex_product(
                complex_product(green_block, source), adjoint(green_block)
            )
            kept_blocks[position] = boundary
            corner = leading(green_block, lesser_block)
        return (jnp.stack(kept_blocks, 2), corner)

    def ascending(section_number):
        return section_number

    def descending(section_number):
        return dom_count - 1 - section_number

    zeros_out = jnp.zeros((4, local_energies, interface, interface), jnp.float32)
    zeros_bounds = jnp.zeros((4, local_energies, local_blocks, interface, interface), jnp.float32)

    def left_runner(inbound):
        return left_sweep(inbound)

    runners = [left_runner, right_sweep]
    orderings = [ascending, descending]
    senders = [pass_right, pass_left]
    stores = [zeros_bounds, zeros_bounds]
    outbounds = [zeros_out, zeros_out]

    def advance(section_number, stores, inbounds, outbounds):
        new_stores = []
        new_outbounds = []
        for chain_number in range(len(runners)):
            active = dom_index == orderings[chain_number](section_number)
            settled = settle(
                runners[chain_number],
                stores[chain_number],
                inbounds[chain_number],
                outbounds[chain_number],
                active,
            )
            new_stores.append(settled[0])
            new_outbounds.append(settled[1])
        return (new_stores, new_outbounds)

    def turn(section_number, loop_state):
        stores, inbounds, outbounds = loop_state
        stores, outbounds = advance(section_number, stores, inbounds, outbounds)
        inbounds = [
            senders[chain_number](outbounds[chain_number]) for chain_number in range(len(runners))
        ]
        return (stores, inbounds, outbounds)

    inbounds = [jnp.zeros_like(outbound) for outbound in outbounds]
    stores, inbounds, outbounds = lax.fori_loop(
        0, dom_count - 1, turn, (stores, inbounds, outbounds)
    )
    stores, outbounds = advance(dom_count - 1, stores, inbounds, outbounds)
    left_store, right_store = stores
    position = 0
    left_part = left_store[:, :, position]
    right_part = right_store[:, :, position]
    matrix, source = system(position)
    matrix = (
        matrix[0] - pad_first(left_part[0], orbitals) - pad_last(right_part[0], orbitals),
        matrix[1] - pad_first(left_part[1], orbitals) - pad_last(right_part[1], orbitals),
    )
    source = (
        source[0] + pad_first(left_part[2], orbitals) + pad_last(right_part[2], orbitals),
        source[1] + pad_first(left_part[3], orbitals) + pad_last(right_part[3], orbitals),
    )
    green_block = inverted(matrix)
    lesser_block = complex_product(complex_product(green_block, source), adjoint(green_block))
    kept_final = [jnp.stack([green_block[0], green_block[1], lesser_block[0], lesser_block[1]])]
    final_store = jnp.stack(kept_final, 2)
    green_real = final_store[0]
    green_imag = final_store[1]
    lesser_real = final_store[2]
    lesser_imag = final_store[3]
    greater_real = lesser_real + green_real - transposed(green_real)
    greater_imag = lesser_imag + green_imag + transposed(green_imag)
    shift_amount = phonon_shift[0]
    quantum_limit = min(2**QUANTUM_BITS, total_energies // 2)
    bit_count = (quantum_limit - 1).bit_length()

    def moved_by(payload, direction):
        for bit_number in range(bit_count):
            amount = direction * 2**bit_number
            remainder = amount % energy_count
            carried = amount // energy_count
            arrived = from_behind(payload, "energy", remainder)
            aligned = jnp.where(
                energy_index < remainder,
                jnp.roll(arrived, carried + 1, axis=1),
                jnp.roll(arrived, carried, axis=1),
            )
            chosen = jnp.right_shift(shift_amount, bit_number) & 1 == 1
            payload = jnp.where(chosen, aligned, payload)
        return payload

    payload = jnp.stack([lesser_real, lesser_imag, greater_real, greater_imag])
    below = moved_by(payload, 1)
    above = moved_by(payload, -1)
    below_lesser = (below[0], below[1])
    below_greater = (below[2], below[3])
    above_lesser = (above[0], above[1])
    above_greater = (above[2], above[3])
    below_source = global_energy - shift_amount
    above_source = global_energy + shift_amount
    valid_below = ((below_source >= 0) & (below_source < total_energies)).astype(jnp.float32)[
        :, None, None, None
    ]
    valid_above = ((above_source >= 0) & (above_source < total_energies)).astype(jnp.float32)[
        :, None, None, None
    ]
    lesser_out_real = phonon_strength * (
        (phonon_bose + 1.0) * (above_lesser[0] * valid_above)
        + phonon_bose * (below_lesser[0] * valid_below)
    )
    lesser_out_imag = phonon_strength * (
        (phonon_bose + 1.0) * (above_lesser[1] * valid_above)
        + phonon_bose * (below_lesser[1] * valid_below)
    )
    greater_out_real = phonon_strength * (
        (phonon_bose + 1.0) * (below_greater[0] * valid_below)
        + phonon_bose * (above_greater[0] * valid_above)
    )
    greater_out_imag = phonon_strength * (
        (phonon_bose + 1.0) * (below_greater[1] * valid_below)
        + phonon_bose * (above_greater[1] * valid_above)
    )
    lesser_out = jnp.stack([lesser_out_real, lesser_out_imag], 2)[:, None]
    greater_out = jnp.stack([greater_out_real, greater_out_imag], 2)[:, None]
    return (lesser_out, greater_out)


MESH = pl.DeviceIdType.MESH
ROWS_BY_ROWS = (((1,), (1,)), ((), ()))
ROWS_BY_COLUMNS = (((1,), (0,)), ((), ()))


def dot(first, second, dims=ROWS_BY_COLUMNS):
    return lax.dot_general(
        first, second, dims, precision=highest, preferred_element_type=jnp.float32
    )


def lanes_of(array):
    return lax.broadcasted_iota(jnp.int32, array.shape, 1)


def times_i(wide):
    half = wide.shape[1] // 2
    moved = pltpu.roll(wide, half, 1)
    return jnp.where(lanes_of(wide) < half, -moved, moved)


def embedded(wide):
    return jnp.concatenate([wide, times_i(wide)], 0)


def wide_product(first, second):
    return dot(first, embedded(second))


def wide_product_adjoint(first, second):
    return dot(first, embedded(second), ROWS_BY_ROWS)


def twice_diagonal(matrix):
    zero = jnp.zeros_like(matrix)
    return jnp.concatenate(
        [jnp.concatenate([matrix, zero], 1), jnp.concatenate([zero, matrix], 1)], 0
    )


def sandwiched(matrix, wide):
    return dot(dot(matrix, wide), twice_diagonal(matrix), ROWS_BY_ROWS)


def scaled_row(real, imag, row):
    plain, turned = row
    return (real * plain + imag * turned, real * turned - imag * plain)


def wide_inverse(wide, group=4):
    size = wide.shape[0]
    rows = lax.broadcasted_iota(jnp.int32, wide.shape, 0)
    lanes = lanes_of(wide)
    row_lanes = lax.broadcasted_iota(jnp.int32, (1, wide.shape[1]), 1)
    for start in range(0, size, group):
        members = range(group)
        in_lanes = (lanes >= start) & (lanes < start + group)
        in_lanes = in_lanes | ((lanes >= size + start) & (lanes < size + start + group))
        in_rows = (rows >= start) & (rows < start + group)
        picked = (row_lanes >= start) & (row_lanes < start + group)
        picked = picked | ((row_lanes >= size + start) & (row_lanes < size + start + group))
        corner, held = [], []
        for member in members:
            row = wide[start + member : start + member + 1, :]
            corner.append(
                [
                    tuple(
                        jnp.broadcast_to(row[:, lane : lane + 1], row.shape)
                        for lane in (start + other, size + start + other)
                    )
                    for other in members
                ]
            )
            turned = jnp.where(picked, 0.0, times_i(row))
            row = jnp.where(picked, 0.0, row)
            row = jnp.where(row_lanes == start + member, 1.0, row)
            turned = jnp.where(row_lanes == size + start + member, 1.0, turned)
            held.append((row, turned))
        for pivot in members:
            real, imag = corner[pivot][pivot]
            scale = 1.0 / (real * real + imag * imag)
            real, imag = real * scale, -imag * scale
            held[pivot] = scaled_row(real, imag, held[pivot])
            for other in range(pivot + 1, group):
                entry = corner[pivot][other]
                corner[pivot][other] = (
                    real * entry[0] - imag * entry[1],
                    real * entry[1] + imag * entry[0],
                )
            for member in members:
                if member == pivot:
                    continue
                real, imag = corner[member][pivot]
                for other in range(pivot + 1, group):
                    entry, kept = corner[pivot][other], corner[member][other]
                    corner[member][other] = (
                        kept[0] - (real * entry[0] - imag * entry[1]),
                        kept[1] - (real * entry[1] + imag * entry[0]),
                    )
                lost = scaled_row(real, imag, held[pivot])
                held[member] = (held[member][0] - lost[0], held[member][1] - lost[1])
        updated = jnp.where(in_rows | in_lanes, 0.0, wide)
        for member in members:
            lane = start + member
            column_real = jnp.broadcast_to(wide[:, lane : lane + 1], wide.shape)
            lane = size + lane
            column_imag = jnp.broadcast_to(wide[:, lane : lane + 1], wide.shape)
            at_member = (rows == start + member).astype(jnp.float32)
            column_real = jnp.where(in_rows, -at_member, column_real)
            column_imag = jnp.where(in_rows, 0.0, column_imag)
            updated = updated - column_real * held[member][0] - column_imag * held[member][1]
        wide = updated
    return wide


def flipped(flag, matrix):
    half = matrix.shape[0] // 2
    moved = pltpu.roll(matrix, half, 1)
    moved = jnp.concatenate([moved[half:], moved[:half]], 0)
    return jnp.where(flag, moved, matrix)


def wide_quarters(real, imag):
    half = real.shape[0] // 2
    left_lanes = lax.broadcasted_iota(jnp.int32, (half, 2 * half), 1) < half
    quarters = []
    for start in (0, half):
        real_rows, imag_rows = real[start : start + half], imag[start : start + half]
        quarters.append(jnp.where(left_lanes, real_rows, pltpu.roll(imag_rows, half, 1)))
        quarters.append(jnp.where(left_lanes, pltpu.roll(real_rows, half, 1), imag_rows))
    return quarters


def real_imag_rows(left, right):
    half = left.shape[0]
    left_lanes = lanes_of(left) < half
    return (
        jnp.where(left_lanes, left, pltpu.roll(right, half, 1)),
        jnp.where(left_lanes, pltpu.roll(left, half, 1), right),
    )


def unit(size):
    rows = lax.broadcasted_iota(jnp.int32, (size, size), 0)
    return (rows == lax.broadcasted_iota(jnp.int32, (size, size), 1)).astype(jnp.float32)


def packed(real, imag):
    rows = lax.broadcasted_iota(jnp.int32, real.shape, 0)
    return jnp.where(rows > lanes_of(real), real, imag)


def pair_kernel(
    numbers,
    hamiltonian,
    coupling,
    rates,
    lesser,
    greater,
    payload,
    outgoing_corners,
    arrived,
    send_sems,
    recv_sems,
):
    place = lax.axis_index("dom")
    partner = 1 - place
    barrier = pltpu.get_barrier_semaphore()
    pl.semaphore_signal(barrier, inc=1, device_id={"dom": partner}, device_id_type=MESH)
    flag = place == 1
    orbitals = hamiltonian.shape[0]
    half = coupling.shape[0]
    identity = unit(orbitals)
    link = coupling[...]
    system_real = (
        numbers[0] * identity
        - 0.5 * (hamiltonian[...] + hamiltonian[...].T)
        - 0.5 * (greater[0] - lesser[0])
    )
    system_imag = broadening * identity - 0.5 * (greater[1] - lesser[1])
    system_real = flipped(flag, system_real)
    system_imag = flipped(flag, system_imag)
    source_real = flipped(flag, lesser[0])
    source_imag = flipped(flag, lesser[1])
    small = unit(half)
    left_gamma = small * rates[0:1, :]
    right_gamma = dot(link * rates[1:2, :], link, ROWS_BY_ROWS)
    gamma = jnp.where(flag, right_gamma, left_gamma)
    zero = jnp.zeros_like(gamma)
    gamma_turned = jnp.concatenate([zero, gamma], 1)
    inner, upper, lower, outer = wide_quarters(system_real, system_imag)
    inner = inner + 0.5 * gamma_turned
    filling = jnp.where(flag, numbers[2], numbers[1])
    gamma_padded = jnp.concatenate([gamma, zero], 1)
    source_imag = source_imag + filling * jnp.concatenate(
        [gamma_padded, jnp.zeros_like(gamma_padded)], 0
    )
    inverse = wide_inverse(inner)
    right = wide_product(inverse, upper)
    left = wide_product(lower, inverse)
    schur = outer - wide_product(left, upper)
    outgoing = jnp.where(flag, small, link.T)
    copies = [
        pltpu.make_async_remote_copy(
            src_ref=outgoing_corners.at[part],
            dst_ref=arrived.at[part],
            send_sem=send_sems.at[part],
            recv_sem=recv_sems.at[part],
            device_id={"dom": partner},
            device_id_type=MESH,
        )
        for part in range(2)
    ]
    first, above, below, last = wide_quarters(source_real, source_imag)
    reduced = last - wide_product(left, above) - wide_product_adjoint(below, left)
    reduced = reduced + wide_product_adjoint(wide_product(left, first), left)
    corner = wide_inverse(schur)
    outgoing_corners[0] = sandwiched(outgoing, corner)
    pl.semaphore_wait(barrier, 1)
    copies[0].start()
    corner_lesser = wide_product_adjoint(wide_product(corner, reduced), corner)
    outgoing_corners[1] = sandwiched(outgoing, corner_lesser)
    copies[1].start()
    incoming = jnp.where(flag, small, link)
    copies[0].wait()
    last = wide_inverse(schur - sandwiched(incoming, arrived[0]))
    lower = wide_product(last, left)
    upper = -wide_product(right, last)
    inner = inverse + wide_product(right, lower)
    top_real, top_imag = real_imag_rows(inner, upper)
    bottom_real, bottom_imag = real_imag_rows(-lower, last)
    green_real = jnp.concatenate([top_real, bottom_real], 0)
    green_imag = jnp.concatenate([top_imag, bottom_imag], 0)
    green = jnp.concatenate([green_real, green_imag], 1)
    copies[1].wait()
    boundary_lesser = sandwiched(incoming, arrived[1])
    added_real, added_imag = real_imag_rows(jnp.zeros_like(boundary_lesser), boundary_lesser)
    source = jnp.concatenate([source_real, source_imag], 1)
    source_bottom = source[half:, :] + jnp.concatenate([added_real, added_imag], 1)
    sources = jnp.concatenate([source[:half, :], source_bottom], 0)
    lesser = wide_product_adjoint(wide_product(green, sources), green)
    lesser_real = flipped(flag, lesser[:, :orbitals])
    lesser_imag = flipped(flag, lesser[:, orbitals:])
    spectral_real = flipped(flag, green_real - green_real.T)
    spectral_imag = flipped(flag, green_imag + green_imag.T)
    payload[0] = packed(lesser_real, lesser_imag)
    payload[1] = packed(lesser_real + spectral_real, lesser_imag + spectral_imag)


def shift_kernel(steps, payload, mixed, below, above, send_sems, recv_sems):
    here = lax.axis_index("energy")
    count = lax.axis_size("energy")
    has_below, has_above = here >= steps, here + steps < count
    lower, higher = jnp.maximum(here - steps, 0), jnp.minimum(here + steps, count - 1)
    barrier = pltpu.get_barrier_semaphore()

    def copy(part, direction):
        slot = 2 * part + direction
        return pltpu.make_async_remote_copy(
            src_ref=payload.at[part],
            dst_ref=(below, above)[direction].at[part],
            send_sem=send_sems.at[slot],
            recv_sem=recv_sems.at[slot],
            device_id={"energy": (higher, lower)[direction]},
            device_id_type=MESH,
        )

    @pl.when(has_below)
    def _():
        pl.semaphore_signal(barrier, inc=1, device_id={"energy": lower}, device_id_type=MESH)

    @pl.when(has_above)
    def _():
        pl.semaphore_signal(barrier, inc=1, device_id={"energy": higher}, device_id_type=MESH)

    @pl.when(jnp.logical_not(has_below))
    def _():
        below[...] = jnp.zeros_like(below)

    @pl.when(jnp.logical_not(has_above))
    def _():
        above[...] = jnp.zeros_like(above)

    pl.semaphore_wait(barrier, has_below.astype(jnp.int32) + has_above.astype(jnp.int32))

    for part in range(2):
        for direction, sends in ((0, has_above), (1, has_below)):
            pl.when(sends)(functools.partial(lambda *at: copy(*at).start(), part, direction))
    emitted = phonon_strength * (phonon_bose + 1.0)
    absorbed = phonon_strength * phonon_bose
    for part, (from_below, from_above) in enumerate(((absorbed, emitted), (emitted, absorbed))):
        for direction, receives in ((0, has_below), (1, has_above)):
            pl.when(receives)(functools.partial(lambda *at: copy(*at).wait_recv(), part, direction))
        mixed[part] = from_below * below[part] + from_above * above[part]
    for part in range(2):
        for direction, sends in ((0, has_above), (1, has_below)):
            pl.when(sends)(functools.partial(lambda *at: copy(*at).wait_send(), part, direction))


def unpack_kernel(mixed, lesser_out, greater_out):
    for part, out in enumerate((lesser_out, greater_out)):
        held = mixed[part]
        rows = lax.broadcasted_iota(jnp.int32, held.shape, 0)
        lanes = lanes_of(held)
        mirrored = held.T
        out[0] = jnp.where(rows > lanes, held, jnp.where(rows < lanes, -mirrored, 0.0))
        out[1] = jnp.where(rows > lanes, mirrored, held)


def vmem(count):
    return [pl.BlockSpec(memory_space=pltpu.VMEM)] * count


def smem(count):
    return [pl.BlockSpec(memory_space=pltpu.SMEM)] * count


def on_pair(hamiltonian, coupling, contact_rates, occupation, lesser_in, greater_in, phonon_shift):
    energy_index = lax.axis_index("energy")
    energy_count = lax.axis_size("energy")
    orbitals = hamiltonian.shape[1]
    half = coupling.shape[1]
    energy_value = -1.5 + 3.0 * energy_index.astype(jnp.float32) / (energy_count - 1)
    numbers = jnp.concatenate([energy_value[None], occupation[0, 0]])
    packed_pair = jax.ShapeDtypeStruct((2, orbitals, orbitals), jnp.float32)
    corners = pltpu.VMEM((2, half, orbitals), jnp.float32)
    payload = pl.pallas_call(
        pair_kernel,
        out_shape=packed_pair,
        in_specs=smem(1) + vmem(5),
        out_specs=vmem(1)[0],
        scratch_shapes=[corners, corners] + [pltpu.SemaphoreType.DMA((2,))] * 2,
        compiler_params=pltpu.CompilerParams(collective_id=0, has_side_effects=True),
    )(
        numbers,
        hamiltonian[0],
        coupling[0],
        contact_rates,
        lesser_in[0, 0, 0],
        greater_in[0, 0, 0],
    )

    def moved(steps, value):
        landing = pltpu.VMEM((2, orbitals, orbitals), jnp.float32)
        return pl.pallas_call(
            functools.partial(shift_kernel, steps),
            out_shape=packed_pair,
            in_specs=vmem(1),
            out_specs=vmem(1)[0],
            scratch_shapes=[landing, landing] + [pltpu.SemaphoreType.DMA((4,))] * 2,
            compiler_params=pltpu.CompilerParams(collective_id=steps, has_side_effects=True),
        )(value)

    limit = min(2**QUANTUM_BITS, energy_count // 2)
    mixed = lax.switch(
        phonon_shift[0] - 1,
        [functools.partial(moved, steps) for steps in range(1, max(limit, 2))],
        payload,
    )
    outs = pl.pallas_call(
        unpack_kernel,
        out_shape=(packed_pair, packed_pair),
        in_specs=vmem(1),
        out_specs=tuple(vmem(2)),
    )(mixed)
    return tuple(out[None, None, None] for out in outs)


def choose(hamiltonian, coupling, contact_rates, occupation, lesser_in, greater_in, phonon_shift):
    pair = lax.axis_size("dom") == 2 and hamiltonian.shape[0] == 1 and occupation.shape[0] == 1
    lanes_fit = hamiltonian.shape[1] == 2 * coupling.shape[1] and hamiltonian.shape[1] % 128 == 0
    program = on_pair if pair and lanes_fit else on_device
    return program(
        hamiltonian, coupling, contact_rates, occupation, lesser_in, greater_in, phonon_shift
    )


def solution(mesh):
    return jax.shard_map(
        choose,
        mesh=mesh,
        in_specs=(
            P("dom", None, None),
            P("dom", None, None),
            P(),
            P(None, "energy", None),
            P(None, "energy", "dom", None, None, None),
            P(None, "energy", "dom", None, None, None),
            P(),
        ),
        out_specs=(
            P(None, "energy", "dom", None, None, None),
            P(None, "energy", "dom", None, None, None),
        ),
        check_vma=False,
    )
```

profile of v0, /device:TPU:0, one launch (start us, length us, event | category | flops | bytes accessed | tf_op | source)
XLA Modules:
  0.0 31.6 jit_solution(17541335069685700933)
XLA Ops:
  1.3 0.0 copy-start
  1.3 0.6 %copy-done = f32[1,1,2]{2,1,0:T(1,128)S(1)} copy-done((f32[1,1,2]{2,1,0:T(1,128)S(1)}, f32[1,1,2]{2,1,0:T(1,128)}, u32[]{:S(2)}) %copy-start) | copy-done | bytes 32
  1.9 0.6 %pad_maximum_fusion.numbers = f32[3]{0:T(128)} fusion(f32[2]{0:T(128)S(1)} %bitcast.15, f32[1]{0:T(128)} %bitcast.1), kind=kLoop, calls=%fused_computation | loop fusion | flops 3 | bytes 24 | tf_op jit(solution)/shard_map/concatenate | solution.py:650
  2.6 20.1 %shard_map.86 = f32[2,128,128]{2,1,0:T(8,128)S(1)} custom-call(f32[3]{0:T(128)} %pad_maximum_fusion.numbers, f32[128,128]{1,0:T(8,128)} %bitcast.11, f32[64,64]{1,0:T(8,128)} %bitcast.12, f32[2,64]{1,0:T(2,128)} %rates.1, f32[2,128,128]{2,1,0:T(8,128)} %bitcast.9, f32[2,128,128]{2,1,0:T(8,128)} %bitcast.10), custom_call_target="tpu_custom_call" | custom-call | tf_op jit(solution)/shard_map/pallas_call | solution.py:653
  22.7 8.1 %conditional.1 = (f32[2,128,128]{2,1,0:T(8,128)S(1)}) conditional(s32[]{:T(128)} %bitcast, f32[2,128,128]{2,1,0:T(8,128)S(1)} %shard_map.86, f32[2,128,128]{2,1,0:T(8,128)S(1)} %shard_map.86, f32[2,128,128]{2,1,0:T(8,128)S(1)} %shard_map.86, f32[2,128,128]{2,1,0:T(8,128)S(1)} %shard_map.86, ...), branch_computations={%region_0.0_spmd, %region_1.0_spmd, %region_2.0_spmd, %region_3.0_... | conditional | bytes 8 | solution.py:681
  22.8 8.1 %branch_6_fun.1 = f32[2,128,128]{2,1,0:T(8,128)S(1)} custom-call(f32[2,128,128]{2,1,0:T(8,128)S(1)} %payload.6), custom_call_target="tpu_custom_call" | custom-call | tf_op jit(solution)/shard_map/cond/branch_6_fun/pallas_call | solution.py:671
  30.8 0.8 %shard_map.87 = (f32[2,128,128]{2,1,0:T(8,128)}, f32[2,128,128]{2,1,0:T(8,128)}) custom-call(f32[2,128,128]{2,1,0:T(8,128)S(1)} %get-tuple-element.21.mixed), custom_call_target="tpu_custom_call" | custom-call | tf_op jit(solution)/shard_map/pallas_call | solution.py:686
Async XLA Ops:
  1.3 0.7 %copy-start = (f32[1,1,2]{2,1,0:T(1,128)S(1)}, f32[1,1,2]{2,1,0:T(1,128)}, u32[]{:S(2)}) copy-start(f32[1,1,2]{2,1,0:T(1,128)} %param.17) | copy-start | bytes 28
where the time goes:
time: 31.8 us; the launch traced here: 31.6 us
  Pallas kernels  29 us (91%)
  between operations  1.31 us (4%)
  local copies, waits for them, and re-layouts  0.65 us (2%)
  other arithmetic  0.65 us (2%)
    pallas_call x1, Pallas kernels, on_pair(): pl.pallas_call(pair_kernel, out_shape=packed_pair, in_specs=smem(1) + vme...  20.1 us
    pallas_call x1, Pallas kernels, moved(): pl.pallas_call(functools.partial(shift_kernel, steps), out_shape=packed_p...  8.07 us
    pallas_call x1, Pallas kernels, on_pair(): pl.pallas_call(unpack_kernel, out_shape=(packed_pair, packed_pair), in_sp...  0.8 us
    unnamed x2, local copies, waits for them, and re-layouts  0.65 us
    concatenate x1, other arithmetic, on_pair(): numbers = jnp.concatenate([energy_value[None], occupation[0, 0]])  0.65 us

commit v1 on v0

--- a/solution.py
+++ b/solution.py
@@ -477,7 +477,7 @@
 
 
 def pair_kernel(
-    numbers,
+    occupation,
     hamiltonian,
     coupling,
     rates,
@@ -486,6 +486,7 @@
     payload,
     outgoing_corners,
     arrived,
+    arrived_link,
     send_sems,
     recv_sems,
 ):
@@ -494,12 +495,14 @@
     barrier = pltpu.get_barrier_semaphore()
     pl.semaphore_signal(barrier, inc=1, device_id={"dom": partner}, device_id_type=MESH)
     flag = place == 1
+    energy_index = lax.axis_index("energy").astype(jnp.float32)
+    energy_value = -1.5 + 3.0 * energy_index / (lax.axis_size("energy") - 1)
     orbitals = hamiltonian.shape[0]
     half = coupling.shape[0]
     identity = unit(orbitals)
     link = coupling[...]
     system_real = (
-        numbers[0] * identity
+        energy_value * identity
         - 0.5 * (hamiltonian[...] + hamiltonian[...].T)
         - 0.5 * (greater[0] - lesser[0])
     )
@@ -516,38 +519,45 @@
     gamma_turned = jnp.concatenate([zero, gamma], 1)
     inner, upper, lower, outer = wide_quarters(system_real, system_imag)
     inner = inner + 0.5 * gamma_turned
-    filling = jnp.where(flag, numbers[2], numbers[1])
+    filling = jnp.where(flag, occupation[:, 1:2], occupation[:, 0:1])
     gamma_padded = jnp.concatenate([gamma, zero], 1)
     source_imag = source_imag + filling * jnp.concatenate(
         [gamma_padded, jnp.zeros_like(gamma_padded)], 0
     )
     inverse = wide_inverse(inner)
-    right = wide_product(inverse, upper)
-    left = wide_product(lower, inverse)
-    schur = outer - wide_product(left, upper)
-    outgoing = jnp.where(flag, small, link.T)
     copies = [
         pltpu.make_async_remote_copy(
-            src_ref=outgoing_corners.at[part],
-            dst_ref=arrived.at[part],
+            src_ref=origin,
+            dst_ref=target,
             send_sem=send_sems.at[part],
             recv_sem=recv_sems.at[part],
             device_id={"dom": partner},
             device_id_type=MESH,
         )
-        for part in range(2)
+        for part, (origin, target) in enumerate(
+            (
+                (outgoing_corners.at[0], arrived.at[0]),
+                (outgoing_corners.at[1], arrived.at[1]),
+                (coupling, arrived_link),
+            )
+        )
     ]
+    pl.semaphore_wait(barrier, 1)
+    copies[2].start()
+    right = wide_product(inverse, upper)
+    left = wide_product(lower, inverse)
+    schur = outer - wide_product(left, upper)
     first, above, below, last = wide_quarters(source_real, source_imag)
     reduced = last - wide_product(left, above) - wide_product_adjoint(below, left)
     reduced = reduced + wide_product_adjoint(wide_product(left, first), left)
     corner = wide_inverse(schur)
-    outgoing_corners[0] = sandwiched(outgoing, corner)
-    pl.semaphore_wait(barrier, 1)
+    outgoing_corners[0] = corner
     copies[0].start()
     corner_lesser = wide_product_adjoint(wide_product(corner, reduced), corner)
-    outgoing_corners[1] = sandwiched(outgoing, corner_lesser)
+    outgoing_corners[1] = corner_lesser
     copies[1].start()
-    incoming = jnp.where(flag, small, link)
+    copies[2].wait()
+    incoming = jnp.where(flag, arrived_link[...].T, link)
     copies[0].wait()
     last = wide_inverse(schur - sandwiched(incoming, arrived[0]))
     lower = wide_product(last, left)
@@ -637,28 +647,22 @@
     return [pl.BlockSpec(memory_space=pltpu.VMEM)] * count
 
 
-def smem(count):
-    return [pl.BlockSpec(memory_space=pltpu.SMEM)] * count
-
-
 def on_pair(hamiltonian, coupling, contact_rates, occupation, lesser_in, greater_in, phonon_shift):
-    energy_index = lax.axis_index("energy")
     energy_count = lax.axis_size("energy")
     orbitals = hamiltonian.shape[1]
     half = coupling.shape[1]
-    energy_value = -1.5 + 3.0 * energy_index.astype(jnp.float32) / (energy_count - 1)
-    numbers = jnp.concatenate([energy_value[None], occupation[0, 0]])
     packed_pair = jax.ShapeDtypeStruct((2, orbitals, orbitals), jnp.float32)
     corners = pltpu.VMEM((2, half, orbitals), jnp.float32)
     payload = pl.pallas_call(
         pair_kernel,
         out_shape=packed_pair,
-        in_specs=smem(1) + vmem(5),
+        in_specs=vmem(6),
         out_specs=vmem(1)[0],
-        scratch_shapes=[corners, corners] + [pltpu.SemaphoreType.DMA((2,))] * 2,
+        scratch_shapes=[corners, corners, pltpu.VMEM((half, half), jnp.float32)]
+        + [pltpu.SemaphoreType.DMA((3,))] * 2,
         compiler_params=pltpu.CompilerParams(collective_id=0, has_side_effects=True),
     )(
-        numbers,
+        occupation[0],
         hamiltonian[0],
         coupling[0],
         contact_rates,

time: 31.8 us -> 28.1 us (0.88)
  Pallas kernels: 29 us -> 26.9 us
  other arithmetic: 0.65 us -> 0 us
  local copies, waits for them, and re-layouts: 0.65 us -> 0 us
    pallas_call x1, Pallas kernels: 20.1 us -> 18.9 us  [on_pair(): pl.pallas_call(pair_kernel, out_shape=packed_pair, in_specs=vmem(6), out_...]
    pallas_call x1, Pallas kernels: 8.07 us -> 7.11 us  [moved(): pl.pallas_call(functools.partial(shift_kernel, steps), out_shape=packed_p...]
    unnamed x2 -> x0, local copies, waits for them, and re-layouts: 0.65 us -> none
    concatenate x1 -> x0, other arithmetic: 0.65 us -> none  [on_pair(): numbers = jnp.concatenate([energy_value[None], occupation[0, 0]])]
where the time goes in v1:
time: 28.1 us; the launch traced here: 28.2 us
  Pallas kernels  26.9 us (96%)
  between operations  1.3 us (5%)
    pallas_call x1, Pallas kernels, on_pair(): pl.pallas_call(pair_kernel, out_shape=packed_pair, in_specs=vmem(6), out_...  18.9 us
    pallas_call x1, Pallas kernels, moved(): pl.pallas_call(functools.partial(shift_kernel, steps), out_shape=packed_p...  7.11 us
    pallas_call x1, Pallas kernels, on_pair(): pl.pallas_call(unpack_kernel, out_shape=(packed_pair, packed_pair), in_sp...  0.8 us

profile of v1, /device:TPU:0, one launch (start us, length us, event | category | flops | bytes accessed | tf_op | source)
XLA Modules:
  0.0 28.2 jit_solution(6695473483726778694)
XLA Ops:
  1.3 18.9 %shard_map.86 = f32[2,128,128]{2,1,0:T(8,128)S(1)} custom-call(f32[1,2]{1,0:T(1,128)} %bitcast.12, f32[128,128]{1,0:T(8,128)} %bitcast.10, f32[64,64]{1,0:T(8,128)} %bitcast.11, f32[2,64]{1,0:T(2,128)} %rates.1, f32[2,128,128]{2,1,0:T(8,128)} %bitcast.8, f32[2,128,128]{2,1,0:T(8,128)} %bitcast.9), custom_call_target="tpu_custom_call" | custom-call | tf_op jit(solution)/shard_map/pallas_call | solution.py:656
  20.2 7.2 %conditional.1 = (f32[2,128,128]{2,1,0:T(8,128)S(1)}) conditional(s32[]{:T(128)} %bitcast, f32[2,128,128]{2,1,0:T(8,128)S(1)} %shard_map.86, f32[2,128,128]{2,1,0:T(8,128)S(1)} %shard_map.86, f32[2,128,128]{2,1,0:T(8,128)S(1)} %shard_map.86, f32[2,128,128]{2,1,0:T(8,128)S(1)} %shard_map.86, ...), branch_computations={%region_0.0_spmd, %region_1.0_spmd, %region_2.0_spmd, %region_3.0_... | conditional | bytes 8 | solution.py:685
  20.3 7.1 %branch_4_fun.1 = f32[2,128,128]{2,1,0:T(8,128)S(1)} custom-call(f32[2,128,128]{2,1,0:T(8,128)S(1)} %payload.4), custom_call_target="tpu_custom_call" | custom-call | tf_op jit(solution)/shard_map/cond/branch_4_fun/pallas_call | solution.py:675
  27.4 0.8 %shard_map.87 = (f32[2,128,128]{2,1,0:T(8,128)}, f32[2,128,128]{2,1,0:T(8,128)}) custom-call(f32[2,128,128]{2,1,0:T(8,128)S(1)} %get-tuple-element.21.mixed), custom_call_target="tpu_custom_call" | custom-call | tf_op jit(solution)/shard_map/pallas_call | solution.py:690

commit v2 on v1

--- a/solution.py
+++ b/solution.py
@@ -547,12 +547,12 @@
     right = wide_product(inverse, upper)
     left = wide_product(lower, inverse)
     schur = outer - wide_product(left, upper)
+    corner = wide_inverse(schur)
+    outgoing_corners[0] = corner
+    copies[0].start()
     first, above, below, last = wide_quarters(source_real, source_imag)
     reduced = last - wide_product(left, above) - wide_product_adjoint(below, left)
     reduced = reduced + wide_product_adjoint(wide_product(left, first), left)
-    corner = wide_inverse(schur)
-    outgoing_corners[0] = corner
-    copies[0].start()
     corner_lesser = wide_product_adjoint(wide_product(corner, reduced), corner)
     outgoing_corners[1] = corner_lesser
     copies[1].start()
@@ -560,6 +560,8 @@
     incoming = jnp.where(flag, arrived_link[...].T, link)
     copies[0].wait()
     last = wide_inverse(schur - sandwiched(incoming, arrived[0]))
+    copies[1].wait()
+    boundary_lesser = sandwiched(incoming, arrived[1])
     lower = wide_product(last, left)
     upper = -wide_product(right, last)
     inner = inverse + wide_product(right, lower)
@@ -568,8 +570,6 @@
     green_real = jnp.concatenate([top_real, bottom_real], 0)
     green_imag = jnp.concatenate([top_imag, bottom_imag], 0)
     green = jnp.concatenate([green_real, green_imag], 1)
-    copies[1].wait()
-    boundary_lesser = sandwiched(incoming, arrived[1])
     added_real, added_imag = real_imag_rows(jnp.zeros_like(boundary_lesser), boundary_lesser)
     source = jnp.concatenate([source_real, source_imag], 1)
     source_bottom = source[half:, :] + jnp.concatenate([added_real, added_imag], 1)

time: 28.1 us -> 27.8 us (0.989)
  Pallas kernels: 26.9 us -> 26.6 us
    pallas_call x1, Pallas kernels: 18.9 us -> 17.6 us  [on_pair(): pl.pallas_call(pair_kernel, out_shape=packed_pair, in_specs=vmem(6), out_...]
    pallas_call x1, Pallas kernels: 7.11 us -> 8.13 us  [moved(): pl.pallas_call(functools.partial(shift_kernel, steps), out_shape=packed_p...]
where the time goes in v2:
time: 27.8 us; the launch traced here: 27.9 us
  Pallas kernels  26.6 us (96%)
  between operations  1.3 us (5%)
    pallas_call x1, Pallas kernels, on_pair(): pl.pallas_call(pair_kernel, out_shape=packed_pair, in_specs=vmem(6), out_...  17.6 us
    pallas_call x1, Pallas kernels, moved(): pl.pallas_call(functools.partial(shift_kernel, steps), out_shape=packed_p...  8.13 us
    pallas_call x1, Pallas kernels, on_pair(): pl.pallas_call(unpack_kernel, out_shape=(packed_pair, packed_pair), in_sp...  0.8 us

profile of v2, /device:TPU:0, one launch (start us, length us, event | category | flops | bytes accessed | tf_op | source)
XLA Modules:
  0.0 27.9 jit_solution(1093221136288874623)
XLA Ops:
  1.3 17.6 %shard_map.86 = f32[2,128,128]{2,1,0:T(8,128)S(1)} custom-call(f32[1,2]{1,0:T(1,128)} %bitcast.12, f32[128,128]{1,0:T(8,128)} %bitcast.10, f32[64,64]{1,0:T(8,128)} %bitcast.11, f32[2,64]{1,0:T(2,128)} %rates.1, f32[2,128,128]{2,1,0:T(8,128)} %bitcast.8, f32[2,128,128]{2,1,0:T(8,128)} %bitcast.9), custom_call_target="tpu_custom_call" | custom-call | tf_op jit(solution)/shard_map/pallas_call | solution.py:656
  18.9 8.2 %conditional.1 = (f32[2,128,128]{2,1,0:T(8,128)S(1)}) conditional(s32[]{:T(128)} %bitcast, f32[2,128,128]{2,1,0:T(8,128)S(1)} %shard_map.86, f32[2,128,128]{2,1,0:T(8,128)S(1)} %shard_map.86, f32[2,128,128]{2,1,0:T(8,128)S(1)} %shard_map.86, f32[2,128,128]{2,1,0:T(8,128)S(1)} %shard_map.86, ...), branch_computations={%region_0.0_spmd, %region_1.0_spmd, %region_2.0_spmd, %region_3.0_... | conditional | bytes 8 | solution.py:685
  19.0 8.1 %branch_5_fun.1 = f32[2,128,128]{2,1,0:T(8,128)S(1)} custom-call(f32[2,128,128]{2,1,0:T(8,128)S(1)} %payload.5), custom_call_target="tpu_custom_call" | custom-call | tf_op jit(solution)/shard_map/cond/branch_5_fun/pallas_call | solution.py:675
  27.1 0.8 %shard_map.87 = (f32[2,128,128]{2,1,0:T(8,128)}, f32[2,128,128]{2,1,0:T(8,128)}) custom-call(f32[2,128,128]{2,1,0:T(8,128)S(1)} %get-tuple-element.21.mixed), custom_call_target="tpu_custom_call" | custom-call | tf_op jit(solution)/shard_map/pallas_call | solution.py:690
